TPU v7x, 32 devices: a whole 2x2x4 slice. The times are simulated.
32 devices in a mesh: box: 16 (over z, y, core), src: 2 (over x).
Axes of the slice: x: 2, y: 2, z: 4, core: 2. Of those that a mesh axis runs over, the one named last changes fastest.
Arguments:
- incident: bfloat16 [128, 256, 256], P('box', 'src'), may hold values from -6 to 6
- reflectivity: float32 [128, 128], P('box'), may hold values from 0.5 to 2
- w_self: bfloat16 [3, 128, 2, 128, 128], P(None, 'box'), may hold values from -0.25 to 0.25
- w_cross: bfloat16 [3, 128, 2, 128, 128], P(None, 'box'), may hold values from -0.25 to 0.25
- receivers: int32 [128], P('box'), may hold values from 0 to 127, as said below
- observed: bfloat16 [128, 256, 256], P('box', 'src'), may hold values from -6 to 6
- group_of: int32 [256], P('src'), may hold values from 0 to 15
- deltas: float32 [16], replicated, may hold values from 0.5 to 4
Outputs:
- image_grad: float32 [128, 128], P('box', 'src')
Inputs may be any that keep to these rules, and one draw needn't show every extreme that they name: `receivers`: trace t lies in box block t // 8, that is between (8 * (t // 8)) and (8 * (t // 8) + 7).
All inputs are finite; a program needn't handle non-finite values.
Results may differ from a plain program's by a relative error of at most 0.001.
Values may be sent and summed in bfloat16 or wider, within the bound.
A program may use at most 64 MiB of HBM per device.

v0:
```python
import jax
import jax.numpy as jnp
from jax import lax
from jax.sharding import PartitionSpec as P


def from_partner(x, axis, distance):
    return lax.ppermute(x, axis, [(i, i ^ 1 << distance) for i in range(lax.axis_size(axis))])


def block_form(weights):
    real_part = weights[:, 0]
    imag_part = weights[:, 1]
    upper_rows = jnp.concatenate([real_part, imag_part], axis=2)
    lower_rows = jnp.concatenate([-imag_part, real_part], axis=2)
    return jnp.concatenate([upper_rows, lower_rows], axis=1)


def forward_apply(values, block):
    return jnp.einsum("bsi,bij->bsj", values, block, preferred_element_type=jnp.float32)


def adjoint_apply(values, block):
    return jnp.einsum("bsj,bij->bsi", values, block, preferred_element_type=jnp.float32)


def body(incident, reflectivity, w_self, w_cross, receivers, observed, group_of, deltas):
    box_count = incident.shape[0]
    sections = w_self.shape[0]
    top_bit = lax.axis_size("box").bit_length() - 1
    block_start = lax.axis_index("box") * box_count
    onehot = (
        (receivers - block_start)[:, None] == jnp.arange(box_count, dtype=jnp.int32)[None, :]
    ).astype(jnp.bfloat16)
    doubled = jnp.concatenate([reflectivity, reflectivity], axis=1)
    wavefield = (doubled[:, None, :] * incident.astype(jnp.float32)).astype(jnp.bfloat16)
    self_blocks = []
    cross_blocks = []
    predicted = None
    for section_idx in range(sections):
        swap_bit = top_bit - 1 - section_idx
        self_block = block_form(w_self[section_idx])
        cross_block = block_form(w_cross[section_idx])
        self_blocks.append(self_block)
        cross_blocks.append(cross_block)
        partner_field = from_partner(wavefield, "box", swap_bit)
        summed = forward_apply(wavefield, self_block) + forward_apply(partner_field, cross_block)
        wavefield = summed.astype(jnp.bfloat16)
    predicted = jnp.einsum("kb,bsi->ksi", onehot, wavefield, preferred_element_type=jnp.float32)
    residual = predicted - observed.astype(jnp.float32)
    node_count = residual.shape[2] // 2
    magnitude = residual[..., :node_count] ** 2 + residual[..., node_count:] ** 2
    group_hits = (
        group_of[:, None] == jnp.arange(deltas.shape[0], dtype=jnp.int32)[None, :]
    ).astype(jnp.float32)
    scale_src = jnp.sum(group_hits * deltas[None, :], axis=1)
    damping = 1.0 / jnp.sqrt(1.0 + magnitude / scale_src[None, :, None] ** 2)
    adj_traces = (residual * jnp.concatenate([damping, damping], axis=2)).astype(jnp.bfloat16)
    adjoint_field = jnp.einsum(
        "kb,ksi->bsi", onehot, adj_traces, preferred_element_type=jnp.float32
    ).astype(jnp.bfloat16)
    for section_idx in reversed(range(sections)):
        swap_bit = top_bit - 1 - section_idx
        outgoing = adjoint_apply(adjoint_field, cross_blocks[section_idx]).astype(jnp.bfloat16)
        received = from_partner(outgoing, "box", swap_bit)
        summed = adjoint_apply(adjoint_field, self_blocks[section_idx]) + received.astype(
            jnp.float32
        )
        adjoint_field = summed.astype(jnp.bfloat16)
    products = incident.astype(jnp.float32) * adjoint_field.astype(jnp.float32)
    image_local = jnp.sum(products[..., :node_count] + products[..., node_count:], axis=1)
    image_summed = lax.psum(image_local, "src")
    share = node_count // lax.axis_size("src")
    return lax.dynamic_slice_in_dim(image_summed, lax.axis_index("src") * share, share, 1)


def solution(mesh):
    in_specs = (
        P("box", "src", None),
        P("box", None),
        P(None, "box", None, None, None),
        P(None, "box", None, None, None),
        P("box"),
        P("box", "src", None),
        P("src"),
        P(),
    )
    out_specs = P("box", "src")
    return jax.shard_map(body, mesh=mesh, in_specs=in_specs, out_specs=out_specs, check_vma=False)
```

profile of v0, /device:TPU:0, one launch (start us, length us, event | category | flops | bytes accessed | tf_op | source)
XLA Modules:
  0.0 116.3 jit_solution(12755048630114793018)
XLA Ops:
  0.0 0.8 pad_maximum_fusion
  0.8 1.1 fusion.5
  1.9 4.1 %collective-permute-start = (bf16[8,128,256]{2,1,0:T(8,128)(2,1)S(1)}, bf16[8,128,256]{2,1,0:T(8,128)(2,1)}, u32[]{:S(2)}, u32[]{:S(2)}) collective-permute-start(bf16[8,128,256]{2,1,0:T(8,128)(2,1)S(1)} %fusion.5), channel_id=1, source_target_pairs={{0,16},{2,18},{4,20},{6,22},{8,24},{10,26},{12,28},{14,30},{16,0},... | collective-permute-start | bytes 1572872 | tf_op jit(solution)/shard_map/ppermute | solution.py:8
  6.0 1.5 %fusion.48 = (bf16[1,8,2,128,128]{4,3,2,1,0:T(8,128)(2,1)S(1)}, bf16[1,8,2,128,128]{4,3,2,1,0:T(8,128)(2,1)S(1)}, bf16[1,8,2,128,128]{4,3,2,1,0:T(8,128)(2,1)S(1)}) fusion(bf16[3,8,2,128,128]{4,3,2,1,0:T(8,128)(2,1)} %param.10), kind=kLoop, calls=%fused_computation.89 | loop fusion | bytes 3145728 | tf_op jit(solution)/shard_map/slice | solution.py:42
  7.5 0.8 slice_bitcast_fusion.10
  8.4 0.7 copy-done
  9.3 0.8 slice_bitcast_fusion.8
  10.2 0.9 slice_bitcast_fusion.6
  11.3 0.7 fusion.47
  12.1 1.5 %fusion.22 = f32[8,128,256]{2,1,0:T(8,128)S(1)} fusion(bf16[8,128,256]{2,1,0:T(8,128)(2,1)S(1)} %fusion.5, bf16[8,128,128]{2,1,0:T(8,128)(2,1)} %get-tuple-element.22, bf16[8,128,128]{2,1,0:T(8,128)(2,1)S(1)} %fusion.42, bf16[8,128,128]{2,1,0:T(8,128)(2,1)} %get-tuple-element.21), kind=kOutput, calls=%fused_computation.47 | convolution fusion | flops 138412032 | bytes 2359296 | tf_op jit(solution)/shard_map/bsi,bij->bsj/dot_general | solution.py:20
  13.6 15.7 %collective-permute-done = bf16[8,128,256]{2,1,0:T(8,128)(2,1)} collective-permute-done((bf16[8,128,256]{2,1,0:T(8,128)(2,1)S(1)}, bf16[8,128,256]{2,1,0:T(8,128)(2,1)}, u32[]{:S(2)}, u32[]{:S(2)}) %collective-permute-start) | collective-permute-done | bytes 524320 | tf_op jit(solution)/shard_map/ppermute | solution.py:8
  29.3 1.4 %fusion = bf16[8,128,256]{2,1,0:T(8,128)(2,1)S(1)} fusion(f32[8,128,256]{2,1,0:T(8,128)S(1)} %fusion.22, bf16[8,128,256]{2,1,0:T(8,128)(2,1)} %collective-permute-done, bf16[8,128,128]{2,1,0:T(8,128)(2,1)S(1)} %copy-done.7, bf16[8,128,128]{2,1,0:T(8,128)(2,1)S(1)} %fusion.43, bf16[8,128,128]{2,1,0:T(8,128)(2,1)S(1)} %copy-done.6), kind=kOutput, calls=%fused_computation.7 | convolution fusion | flops 138936320 | bytes 2883584 | tf_op jit(solution)/shard_map/bsi,bij->bsj/dot_general | solution.py:20
  30.7 0.7 collective-permute-start.1
  31.8 12.1 %collective-permute-done.1 = bf16[8,128,256]{2,1,0:T(8,128)(2,1)S(1)} collective-permute-done((bf16[8,128,256]{2,1,0:T(8,128)(2,1)S(1)}, bf16[8,128,256]{2,1,0:T(8,128)(2,1)S(1)}, u32[]{:S(2)}, u32[]{:S(2)}) %collective-permute-start.1) | collective-permute-done | bytes 524320 | tf_op jit(solution)/shard_map/ppermute | solution.py:8
  44.2 1.3 %collective-permute-start.2 = (bf16[8,128,256]{2,1,0:T(8,128)(2,1)S(1)}, bf16[8,128,256]{2,1,0:T(8,128)(2,1)S(1)}, u32[]{:S(2)}, u32[]{:S(2)}) collective-permute-start(bf16[8,128,256]{2,1,0:T(8,128)(2,1)S(1)} %fusion.1), channel_id=1, source_target_pairs={{0,4},{2,6},{4,0},{6,2},{8,12},{10,14},{12,8},{14,10},{16,20},{18,... | collective-permute-start | bytes 1572872 | tf_op jit(solution)/shard_map/ppermute | solution.py:8
  46.0 10.4 %collective-permute-done.2 = bf16[8,128,256]{2,1,0:T(8,128)(2,1)S(1)} collective-permute-done((bf16[8,128,256]{2,1,0:T(8,128)(2,1)S(1)}, bf16[8,128,256]{2,1,0:T(8,128)(2,1)S(1)}, u32[]{:S(2)}, u32[]{:S(2)}) %collective-permute-start.2) | collective-permute-done | bytes 524320 | tf_op jit(solution)/shard_map/ppermute | solution.py:8
  56.8 0.7 copy-done.2
  57.5 1.4 %convolution_subtract_fusion = f32[8,128,256]{2,0,1:T(8,128)S(1)} fusion(f32[8,128,256]{2,1,0:T(8,128)S(1)} %fusion.20, f32[8,128,256]{2,1,0:T(8,128)S(1)} %fusion.23, bf16[8,128,256]{2,1,0:T(8,128)(2,1)S(1)} %copy-done.2, s32[8]{0:T(128)S(1)} %broadcast_subtract_fusion), kind=kOutput, calls=%fused_computation.2 | convolution fusion | flops 5242944 | bytes 3670048 | tf_op jit(solution)/shard_map/kb,bsi->ksi/dot_general | solution.py:49
  59.4 0.5 convolution_convert_fusion.2
  59.9 1.3 %collective-permute-start.3 = (bf16[8,128,256]{2,1,0:T(8,128)(2,1)S(1)}, bf16[8,128,256]{2,1,0:T(8,128)(2,1)S(1)}, u32[]{:S(2)}, u32[]{:S(2)}) collective-permute-start(bf16[8,128,256]{2,1,0:T(8,128)(2,1)S(1)} %convolution_convert_fusion.2), channel_id=1, source_target_pairs={{0,4},{2,6},{4,0},{6,2},{8,12},{10,14},{12,8},{14,10},{16,20},{18,... | collective-permute-start | bytes 1572872 | tf_op jit(solution)/shard_map/ppermute | solution.py:8
  61.2 10.1 %collective-permute-done.3 = bf16[8,128,256]{2,1,0:T(8,128)(2,1)S(1)} collective-permute-done((bf16[8,128,256]{2,1,0:T(8,128)(2,1)S(1)}, bf16[8,128,256]{2,1,0:T(8,128)(2,1)S(1)}, u32[]{:S(2)}, u32[]{:S(2)}) %collective-permute-start.3) | collective-permute-done | bytes 524320 | tf_op jit(solution)/shard_map/ppermute | solution.py:8
  71.3 0.5 add_convert_fusion
  71.7 0.5 convolution_convert_fusion.1
  72.2 3.0 %collective-permute-start.4 = (bf16[8,128,256]{2,1,0:T(8,128)(2,1)S(1)}, bf16[8,128,256]{2,1,0:T(8,128)(2,1)S(1)}, u32[]{:S(2)}, u32[]{:S(2)}) collective-permute-start(bf16[8,128,256]{2,1,0:T(8,128)(2,1)S(1)} %convolution_convert_fusion.1), channel_id=1, source_target_pairs={{0,8},{2,10},{4,12},{6,14},{8,0},{10,2},{12,4},{14,6},{16,24},{18,... | collective-permute-start | bytes 1572872 | tf_op jit(solution)/shard_map/ppermute | solution.py:8
  75.2 9.4 %collective-permute-done.4 = bf16[8,128,256]{2,1,0:T(8,128)(2,1)S(1)} collective-permute-done((bf16[8,128,256]{2,1,0:T(8,128)(2,1)S(1)}, bf16[8,128,256]{2,1,0:T(8,128)(2,1)S(1)}, u32[]{:S(2)}, u32[]{:S(2)}) %collective-permute-start.4) | collective-permute-done | bytes 524320 | tf_op jit(solution)/shard_map/ppermute | solution.py:8
  84.7 0.5 fusion.2
  85.2 0.5 convolution_convert_fusion
  85.7 5.3 %collective-permute-start.5 = (bf16[8,128,256]{2,1,0:T(8,128)(2,1)S(1)}, bf16[8,128,256]{2,1,0:T(8,128)(2,1)S(1)}, u32[]{:S(2)}, u32[]{:S(2)}) collective-permute-start(bf16[8,128,256]{2,1,0:T(8,128)(2,1)S(1)} %convolution_convert_fusion), channel_id=1, source_target_pairs={{0,16},{2,18},{4,20},{6,22},{8,24},{10,26},{12,28},{14,30},{16,0},... | collective-permute-start | bytes 1572872 | tf_op jit(solution)/shard_map/ppermute | solution.py:8
  91.0 19.2 %collective-permute-done.5 = bf16[8,128,256]{2,1,0:T(8,128)(2,1)S(1)} collective-permute-done((bf16[8,128,256]{2,1,0:T(8,128)(2,1)S(1)}, bf16[8,128,256]{2,1,0:T(8,128)(2,1)S(1)}, u32[]{:S(2)}, u32[]{:S(2)}) %collective-permute-start.5) | collective-permute-done | bytes 524320 | tf_op jit(solution)/shard_map/ppermute | solution.py:8
  110.2 0.5 convert_multiply_fusion
  110.7 4.9 %psum.7 = f32[8,128]{1,0:T(8,128)S(1)} all-reduce(f32[8,128]{1,0:T(8,128)S(1)} %fusion.10), channel_id=1, replica_groups=mesh['box'=16,'src'=2] {'src'}, use_global_device_ids=true, to_apply=%region_2.0 | all-reduce | flops 1024 | bytes 8192 | tf_op jit(solution)/shard_map/psum | solution.py:72
  115.7 0.7 constant_dynamic-slice_fusion
  (49 shorter events, 2.6 us)
Async XLA Ops:
  1.9 27.4 %collective-permute-start = (bf16[8,128,256]{2,1,0:T(8,128)(2,1)S(1)}, bf16[8,128,256]{2,1,0:T(8,128)(2,1)}, u32[]{:S(2)}, u32[]{:S(2)}) collective-permute-start(bf16[8,128,256]{2,1,0:T(8,128)(2,1)S(1)} %fusion.5), channel_id=1, source_target_pairs={{0,16},{2,18},{4,20},{6,22},{8,24},{10,26},{12,28},{14,30},{16,0},... | collective-permute-start | bytes 1572872 | tf_op jit(solution)/shard_map/ppermute | solution.py:8
  7.5 1.6 %copy-start = (bf16[3,8,2,128,128]{4,3,2,1,0:T(8,128)(2,1)S(1)}, bf16[3,8,2,128,128]{4,3,2,1,0:T(8,128)(2,1)}, u32[]{:S(2)}) copy-start(bf16[3,8,2,128,128]{4,3,2,1,0:T(8,128)(2,1)} %param.11) | copy-start | bytes 4718596
  12.1 17.2 %copy-start.6 = (bf16[8,128,128]{2,1,0:T(8,128)(2,1)S(1)}, bf16[8,128,128]{2,1,0:T(8,128)(2,1)}, u32[]{:S(2)}) copy-start(bf16[8,128,128]{2,1,0:T(8,128)(2,1)} %get-tuple-element.19) | copy-start | bytes 786436
  12.1 17.2 %copy-start.7 = (bf16[8,128,128]{2,1,0:T(8,128)(2,1)S(1)}, bf16[8,128,128]{2,1,0:T(8,128)(2,1)}, u32[]{:S(2)}) copy-start(bf16[8,128,128]{2,1,0:T(8,128)(2,1)} %get-tuple-element.20) | copy-start | bytes 786436
  29.3 2.1 %copy-start.10 = (s32[8]{0:T(128)S(1)}, s32[8]{0:T(128)}, u32[]{:S(2)}) copy-start(s32[8]{0:T(128)} %param.12) | copy-start | bytes 100
  29.3 2.2 %copy-start.8 = (bf16[8,128,128]{2,1,0:T(8,128)(2,1)S(1)}, bf16[8,128,128]{2,1,0:T(8,128)(2,1)}, u32[]{:S(2)}) copy-start(bf16[8,128,128]{2,1,0:T(8,128)(2,1)} %get-tuple-element.17) | copy-start | bytes 786436
  29.3 2.2 %copy-start.9 = (bf16[8,128,128]{2,1,0:T(8,128)(2,1)S(1)}, bf16[8,128,128]{2,1,0:T(8,128)(2,1)}, u32[]{:S(2)}) copy-start(bf16[8,128,128]{2,1,0:T(8,128)(2,1)} %get-tuple-element.18) | copy-start | bytes 786436
  30.7 13.2 %collective-permute-start.1 = (bf16[8,128,256]{2,1,0:T(8,128)(2,1)S(1)}, bf16[8,128,256]{2,1,0:T(8,128)(2,1)S(1)}, u32[]{:S(2)}, u32[]{:S(2)}) collective-permute-start(bf16[8,128,256]{2,1,0:T(8,128)(2,1)S(1)} %fusion), channel_id=1, source_target_pairs={{0,8},{2,10},{4,12},{6,14},{8,0},{10,2},{12,4},{14,6},{16,24},{18,... | collective-permute-start | bytes 1572872 | tf_op jit(solution)/shard_map/ppermute | solution.py:8
  43.9 1.7 %copy-start.11 = (f32[16]{0:T(128)S(1)}, f32[16]{0:T(128)}, u32[]{:S(2)}) copy-start(f32[16]{0:T(128)} %param.15) | copy-start | bytes 196
  43.9 1.7 %copy-start.12 = (s32[128]{0:T(128)S(1)}, s32[128]{0:T(128)}, u32[]{:S(2)}) copy-start(s32[128]{0:T(128)} %param.14) | copy-start | bytes 1540
  44.2 12.3 %collective-permute-start.2 = (bf16[8,128,256]{2,1,0:T(8,128)(2,1)S(1)}, bf16[8,128,256]{2,1,0:T(8,128)(2,1)S(1)}, u32[]{:S(2)}, u32[]{:S(2)}) collective-permute-start(bf16[8,128,256]{2,1,0:T(8,128)(2,1)S(1)} %fusion.1), channel_id=1, source_target_pairs={{0,4},{2,6},{4,0},{6,2},{8,12},{10,14},{12,8},{14,10},{16,20},{18,... | collective-permute-start | bytes 1572872 | tf_op jit(solution)/shard_map/ppermute | solution.py:8
  45.7 10.8 %copy-start.3 = (bf16[8,128,128]{2,1,0:T(8,128)(2,1)S(1)}, bf16[8,128,128]{2,1,0:T(8,128)(2,1)}, u32[]{:S(2)}) copy-start(bf16[8,128,128]{2,1,0:T(8,128)(2,1)} %fusion.47) | copy-start | bytes 786436
  56.5 1.0 copy-start.2
  59.9 11.3 %collective-permute-start.3 = (bf16[8,128,256]{2,1,0:T(8,128)(2,1)S(1)}, bf16[8,128,256]{2,1,0:T(8,128)(2,1)S(1)}, u32[]{:S(2)}, u32[]{:S(2)}) collective-permute-start(bf16[8,128,256]{2,1,0:T(8,128)(2,1)S(1)} %convolution_convert_fusion.2), channel_id=1, source_target_pairs={{0,4},{2,6},{4,0},{6,2},{8,12},{10,14},{12,8},{14,10},{16,20},{18,... | collective-permute-start | bytes 1572872 | tf_op jit(solution)/shard_map/ppermute | solution.py:8
  72.2 12.4 %collective-permute-start.4 = (bf16[8,128,256]{2,1,0:T(8,128)(2,1)S(1)}, bf16[8,128,256]{2,1,0:T(8,128)(2,1)S(1)}, u32[]{:S(2)}, u32[]{:S(2)}) collective-permute-start(bf16[8,128,256]{2,1,0:T(8,128)(2,1)S(1)} %convolution_convert_fusion.1), channel_id=1, source_target_pairs={{0,8},{2,10},{4,12},{6,14},{8,0},{10,2},{12,4},{14,6},{16,24},{18,... | collective-permute-start | bytes 1572872 | tf_op jit(solution)/shard_map/ppermute | solution.py:8
  85.1 25.0 %copy-start.1 = (bf16[8,128,256]{2,1,0:T(8,128)(2,1)S(1)}, bf16[8,128,256]{2,1,0:T(8,128)(2,1)}, u32[]{:S(2)}) copy-start(bf16[8,128,256]{2,1,0:T(8,128)(2,1)} %param.8) | copy-start | bytes 1572868
  85.2 25.0 %copy-start.4 = (bf16[8,128,128]{2,1,0:T(8,128)(2,1)S(1)}, bf16[8,128,128]{2,1,0:T(8,128)(2,1)}, u32[]{:S(2)}) copy-start(bf16[8,128,128]{2,1,0:T(8,128)(2,1)} %get-tuple-element.21) | copy-start | bytes 786436
  85.2 25.0 %copy-start.5 = (bf16[8,128,128]{2,1,0:T(8,128)(2,1)S(1)}, bf16[8,128,128]{2,1,0:T(8,128)(2,1)}, u32[]{:S(2)}) copy-start(bf16[8,128,128]{2,1,0:T(8,128)(2,1)} %get-tuple-element.22) | copy-start | bytes 786436
  85.7 24.5 %collective-permute-start.5 = (bf16[8,128,256]{2,1,0:T(8,128)(2,1)S(1)}, bf16[8,128,256]{2,1,0:T(8,128)(2,1)S(1)}, u32[]{:S(2)}, u32[]{:S(2)}) collective-permute-start(bf16[8,128,256]{2,1,0:T(8,128)(2,1)S(1)} %convolution_convert_fusion), channel_id=1, source_target_pairs={{0,16},{2,18},{4,20},{6,22},{8,24},{10,26},{12,28},{14,30},{16,0},... | collective-permute-start | bytes 1572872 | tf_op jit(solution)/shard_map/ppermute | solution.py:8
where the time goes:
time: 117 us; the launch traced here: 116 us
  waiting for transfers between devices  76.9 us (66%)
  starting transfers between devices  15.7 us (13%)
  matrix products  8.72 us (7%)
  local copies, waits for them, and re-layouts  6.59 us (6%)
  blocking collectives  4.95 us (4%)
  other arithmetic  3.17 us (3%)
    ppermute x6, waiting for transfers between devices, from_partner(): lax.ppermute(x, axis, [(i, i ^ 1 << distance) for i in range(lax.axis_siz...  76.9 us
    ppermute x6, starting transfers between devices, from_partner(): lax.ppermute(x, axis, [(i, i ^ 1 << distance) for i in range(lax.axis_siz...  15.7 us
    psum x1, blocking collectives, body(): image_summed = lax.psum(image_local, 'src')  4.95 us
    dot_general x6, matrix products, forward_apply(): jnp.einsum('bsi,bij->bsj', values, block, preferred_element_type=jnp.floa...  4.18 us
    dot_general x6, matrix products, adjoint_apply(): jnp.einsum('bsj,bij->bsi', values, block, preferred_element_type=jnp.floa...  2.86 us
    squeeze x6, local copies, waits for them, and re-layouts, block_form(): imag_part = weights[:, 1]  2.63 us
  transfers between devices with their start and end apart: 6, of which 6 were waited for; matrix products, arithmetic and copies ran while one was open for 7% of the time, Pallas kernels for 0%

commit v1 on v0

v1 whole, which is shorter than its diff:
```python
import functools

import jax
import jax.numpy as jnp
from jax import lax
from jax.experimental import pallas as pl
from jax.experimental.pallas import tpu as pltpu
from jax.sharding import PartitionSpec as P

PARTS = 2
GROUP = 1
LAG = 1
AHEAD = 16
MESH = pl.DeviceIdType.MESH


def rows_by_cols(values, block):
    return lax.dot_general(values, block, (((1,), (0,)), ((), ())), preferred_element_type=jnp.float32)


def rows_by_rows(values, block):
    return lax.dot_general(values, block, (((1,), (1,)), ((), ())), preferred_element_type=jnp.float32)


def kernel(n_box, n_src, inc_hbm, refl_hbm, ws_hbm, wc_hbm, recv_ref, obs_hbm, group_ref, deltas_ref, out_ref,
           inc, pinc, refl, prefl, ws, wc, obs, bs, bc, field, got, inv2, grads, top, cross, back,
           image, image_cross, arrived, local_sem, send_sem, recv_sem, refl_sem, fin_send, fin_recv):
    boxes, sources, width = inc.shape
    nodes = width // 2
    sections = ws.shape[0]
    rows = sources // PARTS
    per_part = boxes // GROUP
    units = PARTS * per_part
    me_box = lax.axis_index("box")
    me_src = lax.axis_index("src")

    def partner(section):
        stride = n_box >> (section + 1)
        return me_box + stride * (1 - 2 * ((me_box // stride) % 2))

    far = partner(0)

    local = [
        pltpu.make_async_copy(ws_hbm, ws, local_sem.at[0]),
        pltpu.make_async_copy(wc_hbm, wc, local_sem.at[1]),
        pltpu.make_async_copy(inc_hbm, inc, local_sem.at[2]),
        pltpu.make_async_copy(refl_hbm, refl, local_sem.at[3]),
        pltpu.make_async_copy(obs_hbm, obs, local_sem.at[4]),
    ]
    for copy in local:
        copy.start()

    barrier = pltpu.get_barrier_semaphore()
    others = [(partner(s), me_src) for s in range(sections)]
    for step in range(1, n_src):
        others.append((me_box, (me_src + step) % n_src))
        others.append((far, (me_src + step) % n_src))
    for other in others:
        pl.semaphore_signal(barrier, inc=1, device_id=other, device_id_type=MESH)
    pl.semaphore_wait(barrier, len(others))

    def place(unit):
        part = unit // per_part
        return pl.multiple_of((unit - part * per_part) * GROUP, GROUP), pl.multiple_of(part * rows, rows)

    def remote(kind, unit):
        box0, row0 = place(unit)
        where = (pl.ds(box0, GROUP), pl.ds(row0, rows))
        if kind == 0:
            source, target, section = inc_hbm.at[where], pinc.at[where], 0
        elif kind < sections:
            source, target, section = field.at[(kind - 1,) + where], got.at[(kind - 1,) + where], kind
        else:
            section = kind - sections + 1
            source, target = cross.at[(section - 1,) + where], back.at[(section - 1,) + where]
        return pltpu.make_async_remote_copy(
            src_ref=source, dst_ref=target, send_sem=send_sem.at[kind, unit], recv_sem=recv_sem.at[kind, unit],
            device_id=(partner(section), me_src), device_id_type=MESH)

    refl_copy = pltpu.make_async_remote_copy(
        src_ref=refl_hbm, dst_ref=prefl, send_sem=refl_sem.at[0], recv_sem=refl_sem.at[1],
        device_id=(far, me_src), device_id_type=MESH)
    refl_copy.start()

    @pl.loop(0, min(AHEAD, units))
    def _(unit):
        remote(0, unit).start()

    scale = jnp.zeros((1, sources), jnp.float32)
    groups = group_ref[...].reshape(1, sources)
    for k in range(deltas_ref.shape[0]):
        scale = jnp.where(groups == k, deltas_ref[k], scale)
    inv2[...] = jnp.broadcast_to(1.0 / (scale * scale), (nodes, sources)).T
    image[...] = jnp.zeros_like(image)
    image_cross[...] = jnp.zeros_like(image_cross)

    for copy in local:
        copy.wait()
    for section in range(sections):
        @pl.loop(0, boxes)
        def _(box):
            for raw, block in ((ws, bs), (wc, bc)):
                real = raw[section, box, 0]
                imag = raw[section, box, 1]
                block[section, box, :nodes, :nodes] = real
                block[section, box, :nodes, nodes:] = imag
                block[section, box, nodes:, :nodes] = -imag
                block[section, box, nodes:, nodes:] = real
    refl_copy.wait_recv()

    def each_box(unit, work):
        box0, row0 = place(unit)
        for i in range(GROUP):
            work(box0 + i, pl.ds(row0, rows))

    def forward(section, unit):
        remote(section, unit).wait_recv()

        def work(box, span):
            if section == 0:
                one = refl[pl.ds(box, 1), :]
                two = prefl[pl.ds(box, 1), :]
                own = (jnp.concatenate([one, one], axis=1) * inc[box, span, :].astype(jnp.float32)).astype(jnp.bfloat16)
                other = (jnp.concatenate([two, two], axis=1) * pinc[box, span, :].astype(jnp.float32)).astype(jnp.bfloat16)
            else:
                own = field[section - 1, box, span, :]
                other = got[section - 1, box, span, :]
            summed = rows_by_cols(own, bs[section, box]) + rows_by_cols(other, bc[section, box])
            field[section, box, span, :] = summed.astype(jnp.bfloat16)

        each_box(unit, work)
        if section < sections - 1:
            remote(section + 1, unit).start()

    def traces(part):
        span = pl.ds(pl.multiple_of(part * rows, rows), rows)

        @pl.loop(0, recv_ref.shape[0])
        def _(t):
            residual = field[sections - 1, lax.rem(recv_ref[t], boxes), span, :].astype(jnp.float32) - obs[t, span, :].astype(jnp.float32)
            magnitude = residual[:, :nodes] ** 2 + residual[:, nodes:] ** 2
            damping = 1.0 / jnp.sqrt(1.0 + magnitude * inv2[span, :])
            grads[t] = (residual * jnp.concatenate([damping, damping], axis=1)).astype(jnp.bfloat16)

        def adjoint_unit(unit):
            def work(box, span):
                total = jnp.zeros((rows, width), jnp.float32)
                for t in range(recv_ref.shape[0]):
                    hit = jnp.where(lax.rem(recv_ref[t], boxes) == box, 1.0, 0.0)
                    total += grads[t].astype(jnp.float32) * hit
                value = total.astype(jnp.bfloat16)
                top[sections - 1, box, span, :] = value
                cross[sections - 2, box, span, :] = rows_by_rows(value, bc[sections - 1, box]).astype(jnp.bfloat16)

            each_box(unit, work)
            remote(2 * sections - 2, unit).start()

        @pl.loop(0, per_part)
        def _(i):
            adjoint_unit(part * per_part + i)

    def adjoint(section, unit):
        remote(sections + section - 1, unit).wait_recv()

        def work(box, span):
            below = rows_by_rows(top[section, box, span, :], bs[section, box]) + back[section - 1, box, span, :].astype(jnp.float32)
            value = below.astype(jnp.bfloat16)
            other = rows_by_rows(value, bc[section - 1, box])
            if section > 1:
                top[section - 1, box, span, :] = value
                cross[section - 2, box, span, :] = other.astype(jnp.bfloat16)
            else:
                own = rows_by_rows(value, bs[0, box])
                for result, term, wave in ((image, own, inc), (image_cross, other, pinc)):
                    product = term * wave[box, span, :].astype(jnp.float32)
                    result[pl.ds(box, 1), :] += jnp.sum(product[:, :nodes] + product[:, nodes:], axis=0, keepdims=True)

        each_box(unit, work)
        if section > 1:
            remote(sections + section - 2, unit).start()

    last = (sections - 1) * LAG
    turn = per_part + last
    steps = units + turn + (sections - 2) * LAG

    @pl.loop(0, steps)
    def _(step):
        if AHEAD < units:
            @pl.when(step + AHEAD < units)
            def _():
                remote(0, step + AHEAD).start()
        for section in range(sections):
            unit = step - section * LAG

            @pl.when((unit >= 0) & (unit < units))
            def _():
                forward(section, unit)
        done = step - last + 1
        part = done // per_part

        @pl.when((done > 0) & (done <= units) & (done == part * per_part))
        def _():
            traces(part - 1)
        for section in range(sections - 1, 0, -1):
            unit = step - turn - (sections - 1 - section) * LAG

            @pl.when((unit >= 0) & (unit < units))
            def _():
                adjoint(section, unit)

    final = []
    for step in range(n_src):
        if step:
            final.append(pltpu.make_async_remote_copy(
                src_ref=image, dst_ref=arrived.at[0, step], send_sem=fin_send.at[0, step], recv_sem=fin_recv.at[0, step],
                device_id=(me_box, (me_src + step) % n_src), device_id_type=MESH))
        final.append(pltpu.make_async_remote_copy(
            src_ref=image_cross, dst_ref=arrived.at[1, step], send_sem=fin_send.at[1, step], recv_sem=fin_recv.at[1, step],
            device_id=(far, (me_src + step) % n_src), device_id_type=MESH))
    for copy in final:
        copy.start()

    refl_copy.wait_send()

    @pl.loop(0, units)
    def _(unit):
        for kind in range(2 * sections - 1):
            remote(kind, unit).wait_send()

    for copy in final:
        copy.wait()
    total = image[...] + arrived[1, 0]
    for step in range(1, n_src):
        total += arrived[0, step] + arrived[1, step]
    share = nodes // n_src
    for k in range(n_src):
        @pl.when(me_src == k)
        def _():
            out_ref[...] = total[:, k * share:(k + 1) * share]


def body(n_box, n_src, incident, reflectivity, w_self, w_cross, receivers, observed, group_of, deltas):
    boxes, sources, width = incident.shape
    nodes = width // 2
    sections = w_self.shape[0]
    units = PARTS * (boxes // GROUP)
    wave = (boxes, sources, width)
    anywhere = pl.BlockSpec(memory_space=pl.ANY)
    scalars = pl.BlockSpec(memory_space=pltpu.SMEM)
    vector = pl.BlockSpec(memory_space=pltpu.VMEM)
    bf16, f32 = jnp.bfloat16, jnp.float32
    return pl.pallas_call(
        functools.partial(kernel, n_box, n_src),
        out_shape=jax.ShapeDtypeStruct((boxes, nodes // n_src), f32),
        in_specs=[anywhere, anywhere, anywhere, anywhere, scalars, anywhere, vector, scalars],
        out_specs=vector,
        scratch_shapes=[
            pltpu.VMEM(wave, bf16),
            pltpu.VMEM(wave, bf16),
            pltpu.VMEM((boxes, nodes), f32),
            pltpu.VMEM((boxes, nodes), f32),
            pltpu.VMEM(w_self.shape, bf16),
            pltpu.VMEM(w_cross.shape, bf16),
            pltpu.VMEM(observed.shape, bf16),
            pltpu.VMEM((sections, boxes, width, width), bf16),
            pltpu.VMEM((sections, boxes, width, width), bf16),
            pltpu.VMEM((sections,) + wave, bf16),
            pltpu.VMEM((sections - 1,) + wave, bf16),
            pltpu.VMEM((sources, nodes), f32),
            pltpu.VMEM((receivers.shape[0], sources // PARTS, width), bf16),
            pltpu.VMEM((sections,) + wave, bf16),
            pltpu.VMEM((sections - 1,) + wave, bf16),
            pltpu.VMEM((sections - 1,) + wave, bf16),
            pltpu.VMEM((boxes, nodes), f32),
            pltpu.VMEM((boxes, nodes), f32),
            pltpu.VMEM((2, n_src, boxes, nodes), f32),
            pltpu.SemaphoreType.DMA((5,)),
            pltpu.SemaphoreType.DMA((2 * sections - 1, units)),
            pltpu.SemaphoreType.DMA((2 * sections - 1, units)),
            pltpu.SemaphoreType.DMA((2,)),
            pltpu.SemaphoreType.DMA((2, n_src)),
            pltpu.SemaphoreType.DMA((2, n_src)),
        ],
        compiler_params=pltpu.CompilerParams(
            collective_id=0, has_side_effects=True, vmem_limit_bytes=56 * 1024 * 1024),
    )(incident, reflectivity, w_self, w_cross, receivers, observed, group_of, deltas)


def solution(mesh):
    in_specs = (
        P("box", "src", None),
        P("box", None),
        P(None, "box", None, None, None),
        P(None, "box", None, None, None),
        P("box"),
        P("box", "src", None),
        P("src"),
        P(),
    )
    run = functools.partial(body, mesh.shape["box"], mesh.shape["src"])
    return jax.shard_map(run, mesh=mesh, in_specs=in_specs, out_specs=P("box", "src"), check_vma=False)
```

time: 117 us -> 94.3 us (0.81)
  Pallas kernels: 0 us -> 92.8 us
  waiting for transfers between devices: 76.9 us -> 0 us
  starting transfers between devices: 15.7 us -> 0 us
  matrix products: 8.72 us -> 0 us
  local copies, waits for them, and re-layouts: 6.59 us -> 1.28 us
  blocking collectives: 4.95 us -> 0 us
  other arithmetic: 3.17 us -> 0 us
    pallas_call x0 -> x1, Pallas kernels: none -> 92.8 us  [body(): pl.pallas_call(functools.partial(kernel, n_box, n_src), out_shape=jax.Sha...]
    ppermute x6 -> x0, waiting for transfers between devices: 76.9 us -> none  [from_partner(): lax.ppermute(x, axis, [(i, i ^ 1 << distance) for i in range(lax.axis_siz...]
    ppermute x6 -> x0, starting transfers between devices: 15.7 us -> none  [from_partner(): lax.ppermute(x, axis, [(i, i ^ 1 << distance) for i in range(lax.axis_siz...]
    dot_general x14 -> x0, matrix products: 8.72 us -> none  [the longest x6 4.18 us: forward_apply(): jnp.einsum('bsi,bij->bsj', values, block, preferred_element_type=jnp.floa...]
    psum x1 -> x0, blocking collectives: 4.95 us -> none  [body(): image_summed = lax.psum(image_local, 'src')]
    squeeze x6 -> x0, local copies, waits for them, and re-layouts: 2.63 us -> none  [block_form(): imag_part = weights[:, 1]]
    slice x2 -> x0, local copies, waits for them, and re-layouts: 1.62 us -> none  [the longest x1 1.48 us: body(): self_block = block_form(w_self[section_idx])]
  transfers between devices with their start and end apart: 6 -> 0, of which waited for: 6 -> 0; matrix products, arithmetic and copies ran while one was open for 7% -> 0% of each run, Pallas kernels for 0% -> 0%
where the time goes in v1:
time: 94.3 us; the launch traced here: 94.1 us
  Pallas kernels  92.8 us (98%)
  local copies, waits for them, and re-layouts  1.28 us (1%)
    pallas_call x1, Pallas kernels, body(): pl.pallas_call(functools.partial(kernel, n_box, n_src), out_shape=jax.Sha...  92.8 us

profile of v1, /device:TPU:0, one launch (start us, length us, event | category | flops | bytes accessed | tf_op | source)
XLA Modules:
  0.0 94.1 jit_solution(18204618443652025763)
XLA Ops:
  0.0 92.8 %shard_map.82 = f32[8,64]{1,0:T(8,128)} custom-call(bf16[8,128,256]{2,1,0:T(8,128)(2,1)} %inc_hbm.1, f32[8,128]{1,0:T(8,128)} %refl_hbm.1, bf16[3,8,2,128,128]{4,3,2,1,0:T(8,128)(2,1)} %ws_hbm.1, bf16[3,8,2,128,128]{4,3,2,1,0:T(8,128)(2,1)} %wc_hbm.1, s32[8]{0:T(128)} %recv_ref.1, bf16[8,128,256]{2,1,0:T(8,128)(2,1)} %obs_hbm.1, s32[128]{0:T(128)} %group_ref.1, ...), custom_call_target="tpu_custom_call" | custom-call | tf_op jit(solution)/shard_map/pallas_call | solution.py:252
  92.8 1.3 %copy.10 = f32[8,64]{1,0:T(8,128)} copy(f32[8,64]{1,0:T(8,128)} %shard_map.82) | data formatting | bytes 4096

commit v2 on v1

--- a/solution.py
+++ b/solution.py
@@ -7,10 +7,10 @@
 from jax.experimental.pallas import tpu as pltpu
 from jax.sharding import PartitionSpec as P
 
-PARTS = 2
-GROUP = 1
-LAG = 1
-AHEAD = 16
+PARTS = 4
+GROUP = 4
+LAG = 2
+AHEAD = 2
 MESH = pl.DeviceIdType.MESH
 
 
@@ -18,12 +18,8 @@
     return lax.dot_general(values, block, (((1,), (0,)), ((), ())), preferred_element_type=jnp.float32)
 
 
-def rows_by_rows(values, block):
-    return lax.dot_general(values, block, (((1,), (1,)), ((), ())), preferred_element_type=jnp.float32)
-
-
 def kernel(n_box, n_src, inc_hbm, refl_hbm, ws_hbm, wc_hbm, recv_ref, obs_hbm, group_ref, deltas_ref, out_ref,
-           inc, pinc, refl, prefl, ws, wc, obs, bs, bc, field, got, inv2, grads, top, cross, back,
+           inc, pinc, refl, prefl, ws, wc, obs, bs, bc, bst, bct, field, got, inv2, grads, top, cross, back,
            image, image_cross, arrived, local_sem, send_sem, recv_sem, refl_sem, fin_send, fin_recv):
     boxes, sources, width = inc.shape
     nodes = width // 2
@@ -108,6 +104,17 @@
                 block[section, box, nodes:, nodes:] = real
     refl_copy.wait_recv()
 
+    def transpose_blocks(box):
+        @pl.loop(0, sections)
+        def _(section):
+            for raw, block in ((ws, bst), (wc, bct)):
+                real = raw[section, box, 0].T
+                imag = raw[section, box, 1].T
+                block[section, box, :nodes, :nodes] = real
+                block[section, box, :nodes, nodes:] = -imag
+                block[section, box, nodes:, :nodes] = imag
+                block[section, box, nodes:, nodes:] = real
+
     def each_box(unit, work):
         box0, row0 = place(unit)
         for i in range(GROUP):
@@ -150,7 +157,7 @@
                     total += grads[t].astype(jnp.float32) * hit
                 value = total.astype(jnp.bfloat16)
                 top[sections - 1, box, span, :] = value
-                cross[sections - 2, box, span, :] = rows_by_rows(value, bc[sections - 1, box]).astype(jnp.bfloat16)
+                cross[sections - 2, box, span, :] = rows_by_cols(value, bct[sections - 1, box]).astype(jnp.bfloat16)
 
             each_box(unit, work)
             remote(2 * sections - 2, unit).start()
@@ -163,14 +170,14 @@
         remote(sections + section - 1, unit).wait_recv()
 
         def work(box, span):
-            below = rows_by_rows(top[section, box, span, :], bs[section, box]) + back[section - 1, box, span, :].astype(jnp.float32)
+            below = rows_by_cols(top[section, box, span, :], bst[section, box]) + back[section - 1, box, span, :].astype(jnp.float32)
             value = below.astype(jnp.bfloat16)
-            other = rows_by_rows(value, bc[section - 1, box])
+            other = rows_by_cols(value, bct[section - 1, box])
             if section > 1:
                 top[section - 1, box, span, :] = value
                 cross[section - 2, box, span, :] = other.astype(jnp.bfloat16)
             else:
-                own = rows_by_rows(value, bs[0, box])
+                own = rows_by_cols(value, bst[0, box])
                 for result, term, wave in ((image, own, inc), (image_cross, other, pinc)):
                     product = term * wave[box, span, :].astype(jnp.float32)
                     result[pl.ds(box, 1), :] += jnp.sum(product[:, :nodes] + product[:, nodes:], axis=0, keepdims=True)
@@ -181,6 +188,7 @@
 
     last = (sections - 1) * LAG
     turn = per_part + last
+    per_step = -(-boxes // turn)
     steps = units + turn + (sections - 2) * LAG
 
     @pl.loop(0, steps)
@@ -195,6 +203,10 @@
             @pl.when((unit >= 0) & (unit < units))
             def _():
                 forward(section, unit)
+        for i in range(per_step):
+            @pl.when(step * per_step + i < boxes)
+            def _():
+                transpose_blocks(step * per_step + i)
         done = step - last + 1
         part = done // per_part
 
@@ -264,6 +276,8 @@
             pltpu.VMEM(observed.shape, bf16),
             pltpu.VMEM((sections, boxes, width, width), bf16),
             pltpu.VMEM((sections, boxes, width, width), bf16),
+            pltpu.VMEM((sections, boxes, width, width), bf16),
+            pltpu.VMEM((sections, boxes, width, width), bf16),
             pltpu.VMEM((sections,) + wave, bf16),
             pltpu.VMEM((sections - 1,) + wave, bf16),
             pltpu.VMEM((sources, nodes), f32),

time: 94.3 us -> 61.7 us (0.65)
  Pallas kernels: 92.8 us -> 60.2 us
    pallas_call x1, Pallas kernels: 92.8 us -> 60.2 us  [body(): pl.pallas_call(functools.partial(kernel, n_box, n_src), out_shape=jax.Sha...]
where the time goes in v2:
time: 61.7 us; the launch traced here: 61.5 us
  Pallas kernels  60.2 us (98%)
  local copies, waits for them, and re-layouts  1.28 us (2%)
    pallas_call x1, Pallas kernels, body(): pl.pallas_call(functools.partial(kernel, n_box, n_src), out_shape=jax.Sha...  60.2 us
    unnamed x1, local copies, waits for them, and re-layouts  1.28 us

profile of v2, /device:TPU:0, one launch (start us, length us, event | category | flops | bytes accessed | tf_op | source)
XLA Modules:
  0.0 61.5 jit_solution(10471364242323872672)
XLA Ops:
  0.0 60.2 %shard_map.82 = f32[8,64]{1,0:T(8,128)} custom-call(bf16[8,128,256]{2,1,0:T(8,128)(2,1)} %inc_hbm.1, f32[8,128]{1,0:T(8,128)} %refl_hbm.1, bf16[3,8,2,128,128]{4,3,2,1,0:T(8,128)(2,1)} %ws_hbm.1, bf16[3,8,2,128,128]{4,3,2,1,0:T(8,128)(2,1)} %wc_hbm.1, s32[8]{0:T(128)} %recv_ref.1, bf16[8,128,256]{2,1,0:T(8,128)(2,1)} %obs_hbm.1, s32[128]{0:T(128)} %group_ref.1, ...), custom_call_target="tpu_custom_call" | custom-call | tf_op jit(solution)/shard_map/pallas_call | solution.py:264
  60.3 1.3 %copy.10 = f32[8,64]{1,0:T(8,128)} copy(f32[8,64]{1,0:T(8,128)} %shard_map.82) | data formatting | bytes 4096

commit v3 on v2

--- a/solution.py
+++ b/solution.py
@@ -11,6 +11,7 @@
 GROUP = 4
 LAG = 2
 AHEAD = 2
+REST = 1
 MESH = pl.DeviceIdType.MESH
 
 
@@ -115,10 +116,12 @@
                 block[section, box, nodes:, :nodes] = imag
                 block[section, box, nodes:, nodes:] = real
 
-    def each_box(unit, work):
+    def each_box(unit, work, keep):
         box0, row0 = place(unit)
+        span = pl.ds(row0, rows)
+        results = [work(box0 + i, span) for i in range(GROUP)]
         for i in range(GROUP):
-            work(box0 + i, pl.ds(row0, rows))
+            keep(box0 + i, span, *results[i])
 
     def forward(section, unit):
         remote(section, unit).wait_recv()
@@ -133,9 +136,12 @@
                 own = field[section - 1, box, span, :]
                 other = got[section - 1, box, span, :]
             summed = rows_by_cols(own, bs[section, box]) + rows_by_cols(other, bc[section, box])
-            field[section, box, span, :] = summed.astype(jnp.bfloat16)
-
-        each_box(unit, work)
+            return (summed.astype(jnp.bfloat16),)
+
+        def keep(box, span, value):
+            field[section, box, span, :] = value
+
+        each_box(unit, work, keep)
         if section < sections - 1:
             remote(section + 1, unit).start()
 
@@ -156,10 +162,13 @@
                     hit = jnp.where(lax.rem(recv_ref[t], boxes) == box, 1.0, 0.0)
                     total += grads[t].astype(jnp.float32) * hit
                 value = total.astype(jnp.bfloat16)
+                return value, rows_by_cols(value, bct[sections - 1, box]).astype(jnp.bfloat16)
+
+            def keep(box, span, value, other):
                 top[sections - 1, box, span, :] = value
-                cross[sections - 2, box, span, :] = rows_by_cols(value, bct[sections - 1, box]).astype(jnp.bfloat16)
-
-            each_box(unit, work)
+                cross[sections - 2, box, span, :] = other
+
+            each_box(unit, work, keep)
             remote(2 * sections - 2, unit).start()
 
         @pl.loop(0, per_part)
@@ -174,21 +183,29 @@
             value = below.astype(jnp.bfloat16)
             other = rows_by_cols(value, bct[section - 1, box])
             if section > 1:
-                top[section - 1, box, span, :] = value
-                cross[section - 2, box, span, :] = other.astype(jnp.bfloat16)
+                return value, other.astype(jnp.bfloat16)
+            own = rows_by_cols(value, bst[0, box])
+            sums = []
+            for term, wave in ((own, inc), (other, pinc)):
+                product = term * wave[box, span, :].astype(jnp.float32)
+                sums.append(jnp.sum(product[:, :nodes] + product[:, nodes:], axis=0, keepdims=True))
+            return sums
+
+        def keep(box, span, first, second):
+            if section > 1:
+                top[section - 1, box, span, :] = first
+                cross[section - 2, box, span, :] = second
             else:
-                own = rows_by_cols(value, bst[0, box])
-                for result, term, wave in ((image, own, inc), (image_cross, other, pinc)):
-                    product = term * wave[box, span, :].astype(jnp.float32)
-                    result[pl.ds(box, 1), :] += jnp.sum(product[:, :nodes] + product[:, nodes:], axis=0, keepdims=True)
-
-        each_box(unit, work)
+                image[pl.ds(box, 1), :] += first
+                image_cross[pl.ds(box, 1), :] += second
+
+        each_box(unit, work, keep)
         if section > 1:
             remote(sections + section - 2, unit).start()
 
     last = (sections - 1) * LAG
-    turn = per_part + last
-    per_step = -(-boxes // turn)
+    turn = per_part + last + REST
+    per_step = -(-boxes // (per_part + last))
     steps = units + turn + (sections - 2) * LAG
 
     @pl.loop(0, steps)

time: 61.7 us -> 59.1 us (0.958)
  Pallas kernels: 60.2 us -> 57.7 us
    pallas_call x1, Pallas kernels: 60.2 us -> 57.7 us  [body(): pl.pallas_call(functools.partial(kernel, n_box, n_src), out_shape=jax.Sha...]
where the time goes in v3:
time: 59.1 us; the launch traced here: 59 us
  Pallas kernels  57.7 us (98%)
  local copies, waits for them, and re-layouts  1.28 us (2%)
    pallas_call x1, Pallas kernels, body(): pl.pallas_call(functools.partial(kernel, n_box, n_src), out_shape=jax.Sha...  57.7 us
    unnamed x1, local copies, waits for them, and re-layouts  1.28 us

profile of v3, /device:TPU:0, one launch (start us, length us, event | category | flops | bytes accessed | tf_op | source)
XLA Modules:
  0.0 59.0 jit_solution(7943731298817674139)
XLA Ops:
  0.0 57.7 %shard_map.82 = f32[8,64]{1,0:T(8,128)} custom-call(bf16[8,128,256]{2,1,0:T(8,128)(2,1)} %inc_hbm.1, f32[8,128]{1,0:T(8,128)} %refl_hbm.1, bf16[3,8,2,128,128]{4,3,2,1,0:T(8,128)(2,1)} %ws_hbm.1, bf16[3,8,2,128,128]{4,3,2,1,0:T(8,128)(2,1)} %wc_hbm.1, s32[8]{0:T(128)} %recv_ref.1, bf16[8,128,256]{2,1,0:T(8,128)(2,1)} %obs_hbm.1, s32[128]{0:T(128)} %group_ref.1, ...), custom_call_target="tpu_custom_call" | custom-call | tf_op jit(solution)/shard_map/pallas_call | solution.py:281
  57.7 1.3 %copy.10 = f32[8,64]{1,0:T(8,128)} copy(f32[8,64]{1,0:T(8,128)} %shard_map.82) | data formatting | bytes 4096
